TPU v7x, 512 devices: a whole 4x4x16 slice. The times are simulated.
512 devices in a mesh: gx: 16 (over y_hi, x, core), gy: 32 (over z, y_lo).
Axes of the slice: x: 4, y: 4 (y_hi: 2, y_lo: 2; y = y_hi * 2 + y_lo), z: 16, core: 2. Of those that a mesh axis runs over, the one named last changes fastest.
Arguments:
- density: float32 [256, 512, 128], P('gx', 'gy'), may hold values from 0.5 to 1.5
- energy: float32 [256, 512, 128], P('gx', 'gy'), may hold values from 1 to 3
- velocity: float32 [3, 256, 512, 128], P(None, 'gx', 'gy'), may hold values from -6 to 6
- mesh_velocity: float32 [3, 256, 512, 128], P(None, 'gx', 'gy'), may hold values from -4 to 4
- density_low: float32 [64, 128, 32], P('gx', 'gy'), may hold values from 0.2 to 0.9
- density_high: float32 [64, 128, 32], P('gx', 'gy'), may hold values from 1.1 to 1.8
- energy_low: float32 [64, 128, 32], P('gx', 'gy'), may hold values from 0.4 to 1.8
- energy_high: float32 [64, 128, 32], P('gx', 'gy'), may hold values from 2.2 to 3.6
Outputs:
- new_density: float32 [256, 512, 128], P('gx', 'gy')
- new_energy: float32 [256, 512, 128], P('gx', 'gy')
- new_velocity: float32 [3, 256, 512, 128], P(None, 'gx', 'gy')
All inputs are finite; a program needn't handle non-finite values.
Results may differ from a plain program's by a relative error of at most 0.0003.
Values sent between devices are 32-bit elements; how exact they have to be, the bound alone decides.
A program may use at most 64 MiB of HBM per device.

v0:
```python
import functools
import math

import jax
import jax.numpy as jnp
import numpy as np
from jax import lax
from jax.experimental import pallas as pl
from jax.experimental.pallas import tpu as pltpu
from jax.sharding import PartitionSpec as P

MESH = pl.DeviceIdType.MESH
F32 = jnp.float32
BF16 = jnp.bfloat16
time_step = 0.02
limit_eps = 1e-06


def lagrange_values(node_set, points):
    result = np.ones((len(points), len(node_set)))
    for column in range(len(node_set)):
        for partner in range(len(node_set)):
            if partner != column:
                result[:, column] = (
                    result[:, column]
                    * (points - node_set[partner])
                    / (node_set[column] - node_set[partner])
                )
    return result


def lagrange_slopes(node_set, points):
    node_total = len(node_set)
    result = np.zeros((len(points), node_total))
    for column in range(node_total):
        for skipped in range(node_total):
            if skipped != column:
                factor = np.ones(len(points)) / (node_set[column] - node_set[skipped])
                for partner in range(node_total):
                    if partner != column and partner != skipped:
                        factor = (
                            factor
                            * (points - node_set[partner])
                            / (node_set[column] - node_set[partner])
                        )
                result[:, column] = result[:, column] + factor
    return result


def basis_tables():
    gauss_points = np.array(
        [-0.8611363115940526, -0.3399810435848563, 0.3399810435848563, 0.8611363115940526]
    )
    gauss_weights = np.array(
        [0.3478548451374538, 0.6521451548625461, 0.6521451548625461, 0.3478548451374538]
    )
    lobatto_points = np.array([-1.0, -math.sqrt(3.0 / 7.0), 0.0, math.sqrt(3.0 / 7.0), 1.0])
    lobatto_weights = np.array([0.1, 49.0 / 90.0, 32.0 / 45.0, 49.0 / 90.0, 0.1])
    slopes = lagrange_slopes(gauss_points, gauss_points)
    volume = (2.0 / gauss_weights)[:, None] * slopes.T * gauss_weights[None, :]
    trace_low = lagrange_values(gauss_points, np.array([-1.0]))[0]
    trace_high = lagrange_values(gauss_points, np.array([1.0]))[0]
    stiffness = (
        2.0 * lobatto_weights[:, None] * lagrange_slopes(lobatto_points, lobatto_points)
    )
    lumped = np.array([0.2, lobatto_weights[1], lobatto_weights[2], lobatto_weights[3], 0.2])
    return {
        "weights": gauss_weights / 2.0,
        "volume": time_step * volume,
        "trace_low": trace_low,
        "trace_high": trace_high,
        "lift_low": time_step * 2.0 * trace_low / gauss_weights,
        "lift_high": time_step * 2.0 * trace_high / gauss_weights,
        "to_points": lagrange_values(lobatto_points, gauss_points),
        "stiffness": -time_step * stiffness / lumped[:, None],
    }


TABLES = basis_tables()
TABLE = {name: TABLES[name].tolist() for name in TABLES}


def lane_matrices(lanes):
    zones = lanes // 4
    shape = (lanes, lanes)
    volume, lift = np.zeros(shape), np.zeros(shape)
    minus, plus = np.zeros(shape), np.zeros(shape)
    stiff, interp = np.zeros(shape), np.zeros(shape)
    pick, spread = np.zeros(shape), np.zeros(shape)
    for zone in range(zones):
        at = 4 * zone
        before = 4 * ((zone - 1) % zones)
        for within in range(4):
            for source in range(4):
                volume[at + source, at + within] = TABLES["volume"][within, source]
                minus[before + source, at + within] = TABLES["trace_high"][source]
                plus[at + source, at + within] = TABLES["trace_low"][source]
            lift[at, at + within] = TABLES["lift_low"][within]
            lift[at, before + within] = -TABLES["lift_high"][within]
            pick[at, at + within] = 1.0
            spread[zone, at + within] = 1.0
            for source in range(5):
                interp[(at + source) % lanes, at + within] += TABLES["to_points"][within, source]
        for target in range(5):
            for source in range(5):
                stiff[(at + source) % lanes, (at + target) % lanes] += TABLES["stiffness"][
                    target, source
                ]
    matrices = [minus, plus, stiff, interp, pick, spread, volume, lift]
    return np.concatenate(matrices, axis=1).astype(np.float32)


def spin(values, steps, axis):
    size = values.shape[axis]
    steps = steps % size
    return values if steps == 0 else pltpu.roll(values, steps, axis)


def rows_of(shape):
    return lax.broadcasted_iota(jnp.int32, shape, len(shape) - 2)


def low_half(shape):
    return rows_of(shape) < 4


def at_zone(shape, zone):
    return rows_of(shape) % 4 == zone


def combine(coefficients, terms):
    total = None
    for factor, term in zip(coefficients, terms):
        part = factor * term
        total = part if total is None else total + part
    return total


def parted(values):
    upper = values.astype(BF16)
    return upper, (values - upper.astype(F32)).astype(BF16)


def product(left, right):
    return jnp.dot(left, right, preferred_element_type=F32)


def mirrored(matrix):
    size = len(matrix[0])
    middle = size // 2
    even = [[(row[c] + row[size - 1 - c]) / 2 for c in range(middle)] for row in matrix]
    odd = [[(row[c] - row[size - 1 - c]) / 2 for c in range(middle)] for row in matrix]
    centre = [row[middle] for row in matrix] if size % 2 else None
    return even, odd, centre


def pairs_of(values):
    size = len(values)
    sums = [values[c] + values[size - 1 - c] for c in range(size // 2)]
    gaps = [values[c] - values[size - 1 - c] for c in range(size // 2)]
    return sums, gaps


def slopes_of(matrix, values):
    even, odd, centre = mirrored(matrix)
    sums, gaps = pairs_of(values)
    size = len(matrix)
    result = [None] * size
    for a in range(size // 2):
        factors, terms = list(even[a]), list(sums)
        if centre is not None:
            factors.append(centre[a])
            terms.append(values[size // 2])
        outer, inner = combine(factors, terms), combine(odd[a], gaps)
        result[a], result[size - 1 - a] = inner + outer, inner - outer
    if size % 2:
        result[size // 2] = combine(odd[size // 2], gaps)
    return result


def points_of(matrix, values):
    even, odd, centre = mirrored(matrix)
    sums, gaps = pairs_of(values)
    result = [None] * 4
    for i in range(2):
        outer = combine(even[i] + [centre[i]], sums + [values[2]])
        inner = combine(odd[i], gaps)
        result[i], result[3 - i] = outer + inner, outer - inner
    return result


def traces_of(values):
    sums, gaps = pairs_of(values)
    even, odd, _ = mirrored([TABLE["trace_low"]])
    outer, inner = combine(even[0], sums), combine(odd[0], gaps)
    return outer + inner, outer - inner


def lifts_of(lower, upper):
    even, odd, _ = mirrored([TABLE["lift_low"]])
    gap, both = lower - upper, lower + upper
    result = [None] * 4
    for i in range(2):
        outer, inner = even[0][i] * gap, odd[0][i] * both
        result[i], result[3 - i] = outer + inner, outer - inner
    return result


def turned(pieces):
    return [jnp.stack([pieces[j][i] for j in range(4)]) for i in range(4)]


def pack_x_low(planes):
    mask = low_half((8, 128))
    return [jnp.where(mask, planes[t], spin(planes[t + 1], 4, 0)) for t in (0, 2)]


def pack_x_high(planes):
    mask = low_half((8, 128))
    return [jnp.where(mask, spin(planes[t], 4, 0), planes[t + 1]) for t in (0, 2)]


def unpack_x_high(packed):
    return [spin(packed[0], 4, 0), packed[0], spin(packed[1], 4, 0), packed[1]]


def unpack_x_low(packed):
    return [packed[0], spin(packed[0], 4, 0), packed[1], spin(packed[1], 4, 0)]


def pack_y(values, start):
    shape = (8, 128)
    packed = []
    for half in range(2):
        total = spin(values[4 * half + 3], 3 - start, 0)
        for place in (2, 1, 0):
            moved = spin(values[4 * half + place], place - start, 0)
            total = jnp.where(at_zone(shape, place), moved, total)
        packed.append(total)
    return packed


def unpack_y(packed, end):
    return jnp.stack([spin(packed, end - place, 0) for place in range(4)])


def kernel(
    counts,
    density, energy, velocity, mesh_velocity, density_low, density_high, energy_low, energy_high,
    tables_hbm,
    results,
    raw_u, raw_v, raw_m, tables, square, ends, picker, tall, bound_in, bound_rows,
    bounds, work_u, work_v, work_m,
    acc_v, sec_v, acc_f, sec_f, speed, face_x, face_y, trace_x, trace_y, ends_z,
    halo_x, halo_y, halo_corner,
    out_dx, out_ux, out_dy, out_uy, in_dx, in_ux, in_dy, in_uy,
    out_corner, in_corner,
    out_dx2, out_ux2, out_dy2, out_uy2, in_dx2, in_ux2, in_dy2, in_uy2,
    load_sem, send_sem, recv_sem,
):
    count_x, count_y = counts
    here_x, here_y = lax.axis_index("gx"), lax.axis_index("gy")
    west = lax.rem(here_x + count_x - 1, count_x)
    east = lax.rem(here_x + 1, count_x)
    south = lax.rem(here_y + count_y - 1, count_y)
    north = lax.rem(here_y + 1, count_y)
    to_west, to_east = (west, here_y), (east, here_y)
    to_south, to_north = (here_x, south), (here_x, north)
    to_corner, from_corner = (west, south), (east, north)

    loads = {}

    def load(name, source, target):
        copy = pltpu.make_async_copy(source, target, load_sem.at[sum(map(len, loads.values()))])
        copy.start()
        loads.setdefault(name, []).append(copy)

    def loaded(name):
        for copy in loads[name]:
            copy.wait()

    places = [(pl.ds(16 * half, 16), pl.ds(8 * half, 8)) for half in range(2)]
    for rows, block in places:
        load("mesh", mesh_velocity.at[:, block], raw_m.at[:, :, rows, :])
        load("velocity", velocity.at[:, block], raw_v.at[:, :, rows, :])
    for rows, block in places:
        load("fields", density.at[block], raw_u.at[0, :, rows, :])
        load("fields", energy.at[block], raw_u.at[1, :, rows, :])

    barrier = pltpu.get_barrier_semaphore()
    for peer in (to_west, to_east, to_south, to_north, to_corner, from_corner):
        pl.semaphore_signal(barrier, inc=1, device_id=peer, device_id_type=MESH)
    load("tables", tables_hbm, tables)
    for index, source in enumerate((density_low, density_high, energy_low, energy_high)):
        load("bounds", source, bound_in.at[index])

    quad, plane = (4, 8, 128), (8, 128)
    low_rows, low_quad = low_half(plane), low_half(quad)
    first_zone, last_zone = at_zone(quad, 0), at_zone(quad, 3)
    stiff, points = TABLE["stiffness"], TABLE["to_points"]
    zero = jnp.zeros(plane, F32)

    def arrange(source, target, which):
        for j in range(4):
            target[which, :, j] = source[which, :, pl.ds(j, 8, stride=4), :]

    def put_pair(target, item, pair):
        target[item, 0] = pair[0]
        target[item, 1] = pair[1]

    def sided(values):
        upper, lower = parted(values)
        return upper, jnp.concatenate([upper, lower], 1)

    def lanes_product(values, column):
        _, pair = sided(values)
        both = product(pair, square[:, 256 * column : 256 * (column + 1)])
        return both[:, :128] + both[:, 128:]

    def picked(values):
        return product(sided(values)[1], picker[...])

    def field_traces(which, source):
        for half in range(2):
            chunk = pl.ds(4 * half, 4)
            low, high = traces_of([source[which, 4 * half + i] for i in range(4)])
            trace_x[which, 0, half], trace_x[which, 1, half] = low, high
            low, high = traces_of([source[which, chunk, j] for j in range(4)])
            trace_y[which, 0, chunk], trace_y[which, 1, chunk] = low, high

    def pack_field(which, item, buffers):
        west_to, east_to, south_to, north_to = buffers
        put_pair(west_to, item, pack_x_low(trace_x[which, 0, 0]))
        put_pair(east_to, item, pack_x_high(trace_x[which, 1, 1]))
        put_pair(south_to, item, pack_y(trace_y[which, 0], 0))
        put_pair(north_to, item, pack_y(trace_y[which, 1], 3))

    def pack_velocity(source, which, offset, buffers):
        item = offset + which
        west_to, east_to, south_to, north_to = buffers
        put_pair(west_to, item, pack_x_low(source[which, 0]))
        closing = combine(stiff[4][:4], [source[which, 4 + a] for a in range(4)])
        put_pair(east_to, item, pack_x_high(closing))
        put_pair(south_to, item, pack_y(source[which, :, 0], 0))
        closing = combine(stiff[4][:4], [source[which, :, j] for j in range(4)])
        put_pair(north_to, item, pack_y(closing, 3))

    leaving_a, leaving_b = (out_dx, out_ux, out_dy, out_uy), (out_dx2, out_ux2, out_dy2, out_uy2)
    arrived_a, arrived_b = (in_dx, in_ux, in_dy, in_uy), (in_dx2, in_ux2, in_dy2, in_uy2)
    loaded("mesh")
    corner = zero
    for which in range(3):
        values = raw_m[which, :, pl.ds(0, 8, stride=4), :]
        put_pair(out_dy, 5 + which, pack_y(values, 0))
        corner = jnp.where(rows_of(plane) == which, spin(values[0], which, 0), corner)
        values = [raw_m[which, 0, pl.ds(j, 8, stride=4), :] for j in range(4)]
        put_pair(out_dx, 5 + which, pack_x_low(values))
    out_corner[...] = corner
    loaded("velocity")
    for which in range(3):
        arrange(raw_v, work_v, which)
        pack_velocity(work_v, which, 2, leaving_a)
    loaded("fields")
    for which in range(2):
        arrange(raw_u, work_u, which)
        field_traces(which, work_u)
        pack_field(which, which, leaving_a)

    pl.semaphore_wait(barrier, 6)
    copies = []
    peers = (to_west, to_east, to_south, to_north)

    def send(source, target, peer):
        copy = pltpu.make_async_remote_copy(
            src_ref=source, dst_ref=target,
            send_sem=send_sem.at[len(copies)], recv_sem=recv_sem.at[len(copies)],
            device_id=peer, device_id_type=MESH,
        )
        copy.start()
        copies.append(copy)
        return copy

    def send_all(sources, targets):
        return [send(*triple) for triple in zip(sources, targets, peers)]

    first = send_all(leaving_a, arrived_a) + [send(out_corner, in_corner, to_corner)]

    loaded("tables")
    minus, plus, stiff_z, interp_z, pick_z, spread_z, volume_z, lift_z = (
        tables[:, 128 * column : 128 * (column + 1)] for column in range(8)
    )
    for column, table in enumerate((stiff_z, interp_z)):
        upper, lower = parted(table)
        at = 256 * column
        square[:128, at : at + 128] = upper
        square[128:, at : at + 128] = upper
        square[:128, at + 128 : at + 256] = lower
        square[128:, at + 128 : at + 256] = jnp.zeros((128, 128), BF16)
    for column, table in enumerate((minus, plus)):
        upper, lower = parted(table)
        at = 128 * column
        ends[:128, at : at + 128] = upper
        ends[128:256, at : at + 128] = upper
        ends[256:, at : at + 128] = lower
    picker[:128] = pick_z.astype(BF16)
    picker[128:] = pick_z.astype(BF16)
    for row, table in enumerate((volume_z, lift_z)):
        upper, lower = parted(table)
        tall[128 * row : 128 * (row + 1), :128] = upper
        tall[128 * row : 128 * (row + 1), 128:] = lower

    loaded("bounds")
    bound_rows[...] = jnp.zeros((4, 2, 8, 128), F32)
    for index in range(4):
        for zone in range(4):
            bound_rows[index, zone % 2, pl.ds(4 * (zone // 2), 4), pl.ds(0, 32)] = bound_in[
                index, zone
            ]
    values = bound_rows[...].reshape(64, 128)
    spreader = spread_z.astype(BF16)
    upper = values.astype(BF16)
    rest = values - upper.astype(F32)
    middle = rest.astype(BF16)
    lowest = (rest - middle.astype(F32)).astype(BF16)
    values = product(upper, spreader) + (product(middle, spreader) + product(lowest, spreader))
    bounds[...] = values.reshape(4, 2, 8, 128)

    def velocity_before(which, source, base):
        along_z = lanes_product(source[which].reshape(256, 128), 0).reshape(8, 4, 8, 128)
        own = stiff[4][4]
        opening = source[which, 0]
        inner = jnp.where(low_quad, spin(opening, 4, 1), 0.0)
        last_end = combine(stiff[4], [source[which, 4 + a] for a in range(4)] + [inner])
        carried = jnp.where(low_quad, own * opening, spin(last_end, 4, 1))
        for half in range(2):
            chunk = pl.ds(4 * half, 4)
            ahead = source[which, 4] if half == 0 else inner
            along_x = slopes_of(stiff, [source[which, 4 * half + a] for a in range(4)] + [ahead])
            along_x[0] = along_x[0] + carried
            carried = along_x[4]
            lines = [source[which, chunk, j] for j in range(4)]
            ahead = jnp.where(last_zone, 0.0, spin(lines[0], 7, 1))
            along_y = slopes_of(stiff, lines + [ahead])
            along_y[0] = along_y[0] + jnp.where(first_zone, own * lines[0], spin(along_y[4], 1, 1))
            along_y = turned(along_y[:4])
            for a in range(4):
                x = 4 * half + a
                acc_v[which, x] = base(x) + (
                    work_m[0, x] * along_x[a]
                    + work_m[1, x] * along_y[a]
                    + work_m[2, x] * along_z[x]
                )

    def velocity_after(which, put, arrived):
        from_east, from_west, from_north, from_south = arrived
        later = jnp.stack(unpack_x_high([from_east[2 + which, 0], from_east[2 + which, 1]]))
        earlier = jnp.stack(unpack_x_low([from_west[2 + which, 0], from_west[2 + which, 1]]))
        later = jnp.where(low_quad, 0.0, later)
        earlier = jnp.where(low_quad, earlier, 0.0)
        for half in range(2):
            above = jnp.where(last_zone, unpack_y(from_north[2 + which, half], 3), 0.0)
            below = jnp.where(first_zone, unpack_y(from_south[2 + which, half], 0), 0.0)
            extra_y = [stiff[j][4] * above for j in range(4)]
            extra_y[0] = extra_y[0] + below
            extra_y = turned(extra_y)
            for a in range(4):
                x = 4 * half + a
                value = acc_v[which, x] + work_m[1, x] * extra_y[a]
                if half == 1:
                    value = value + work_m[0, x] * (stiff[a][4] * later)
                elif a == 0:
                    value = value + work_m[0, x] * earlier
                put(x, value)

    def mesh_before(item):
        values = work_m[min(item, 2)].reshape(256, 128)
        values = lanes_product(values, 1) if item < 3 else picked(values)
        values = values.reshape(8, 4, 8, 128)
        inner = jnp.where(low_quad, spin(values[0], 4, 1), 0.0)
        for half in range(2):
            chunk = pl.ds(4 * half, 4)
            ahead = values[4] if half == 0 else inner
            across = points_of(points, [values[4 * half + a] for a in range(4)] + [ahead])
            across = turned(across)
            ahead = jnp.where(last_zone, 0.0, spin(across[0], 7, 1))
            for j, result in enumerate(points_of(points, across + [ahead])):
                speed[item, chunk, j] = result
            if item == 0:
                edge = values[4 * half]
                ahead = jnp.where(at_zone(plane, 3), 0.0, spin(edge[0], 7, 0))
                edge = points_of(points, [edge[j] for j in range(4)] + [ahead])
                face_x[half] = jnp.stack(edge)
            if item == 1:
                face_y[0, chunk] = across[0]
                face_y[1, chunk] = ahead

    def mesh_halo():
        values = jnp.concatenate(
            [in_dx[5:8].reshape(48, 128), in_dy[5:8].reshape(48, 128), in_corner[...], zero], 0
        )
        both, extra = lanes_product(values, 1), picked(values)
        for item in range(4):
            which, source = min(item, 2), both if item < 3 else extra
            halo_x[item] = source[16 * which : 16 * (which + 1)].reshape(2, 8, 128)
            halo_y[item] = source[48 + 16 * which : 64 + 16 * which].reshape(2, 8, 128)
            halo_corner[item] = spin(source[96:104], 7 - which, 0)

    def mesh_after(item):
        rows = rows_of(plane)
        later = unpack_x_high([halo_x[item, 0], halo_x[item, 1]])
        later = [jnp.where(low_rows, 0.0, value) for value in later]
        far = jnp.where(at_zone(plane, 3), 0.0, spin(later[0], 7, 0))
        far = jnp.where(rows == 7, halo_corner[item], far)
        later.append(jnp.where(low_rows, 0.0, far))
        edge = jnp.stack(points_of(points, later))
        above = [
            jnp.where(last_zone, unpack_y(halo_y[item, half], 3), 0.0) for half in range(2)
        ]
        inner = jnp.where(low_rows, spin(above[0][0], 4, 0), 0.0)
        for half in range(2):
            ahead = above[1][0] if half == 0 else inner
            across = points_of(points, [above[half][a] for a in range(4)] + [ahead])
            for i in range(4):
                x = 4 * half + i
                extra = jnp.stack([points[j][4] * across[i] for j in range(4)])
                if half == 1:
                    extra = extra + points[i][4] * edge
                speed[item, x] += extra
                if item == 1:
                    upper = face_y[1, x] + across[i]
                    if half == 1:
                        upper = upper + points[i][4] * later[4]
                        face_y[0, x] += points[i][4] * later[0]
                    face_y[1, x] = upper
            if item == 0:
                face_x[half] += jnp.stack([points[j][4] * above[half][0] for j in range(4)])
        if item == 0:
            face_x[2] = jnp.where(low_quad, spin(face_x[0], 4, 1), edge)

    def upwind(face, minus_side, plus_side):
        return jnp.maximum(face, 0.0) * minus_side + jnp.minimum(face, 0.0) * plus_side

    def field_ends(which, source):
        upper, pair = sided(source[which].reshape(256, 128))
        sides = product(pair, ends[:256]) + product(upper, ends[256:])
        ends_z[which, 0] = sides[:, :128]
        ends_z[which, 1] = sides[:, 128:]

    def field_before(which, source, base):
        values = source[which].reshape(256, 128)
        flux = upwind(speed[3].reshape(256, 128), ends_z[which, 0], ends_z[which, 1])
        moved = speed[2].reshape(256, 128) * values
        upper, lower = parted(jnp.concatenate([moved, flux], 1))
        sums = product(upper, tall[...])
        along_z = sums[:, :128] + sums[:, 128:] + product(lower, tall[:, :128])
        along_z = along_z.reshape(8, 4, 8, 128)
        for half in range(2):
            chunk = pl.ds(4 * half, 4)
            places = [4 * half + i for i in range(4)]
            along_x = slopes_of(TABLE["volume"], [speed[0, x] * source[which, x] for x in places])
            along_y = slopes_of(
                TABLE["volume"],
                [speed[1, chunk, j] * source[which, chunk, j] for j in range(4)],
            )
            along_y = turned(along_y)
            for i, x in enumerate(places):
                acc_f[which, x] = base(x) + ((along_x[i] + along_y[i]) + along_z[x])

    def in_group(values, join):
        lane = lax.broadcasted_iota(jnp.int32, plane, 1)
        partner = jnp.where(lane % 2 == 0, spin(values, 127, 1), spin(values, 1, 1))
        values = join(values, partner)
        partner = jnp.where(lane // 2 % 2 == 0, spin(values, 126, 1), spin(values, 2, 1))
        return join(values, partner)

    def over_zone(values, join):
        total = functools.reduce(join, values)
        return functools.reduce(join, [total[j] for j in range(4)])

    def limited(which, half, values):
        weights = TABLE["weights"]
        mean = combine(weights, values)
        mean = combine(weights, [mean[j] for j in range(4)])
        lane = lax.broadcasted_iota(jnp.int32, plane, 1) % 4
        middle = (lane == 1) | (lane == 2)
        mean = in_group(mean * jnp.where(middle, weights[1], weights[0]), jnp.add)
        rise = in_group(over_zone(values, jnp.maximum), jnp.maximum) - mean
        fall = in_group(over_zone(values, jnp.minimum), jnp.minimum) - mean
        low, high = bounds[2 * which, half], bounds[2 * which + 1, half]
        theta = jnp.minimum(
            (high - mean) / (rise + limit_eps), (mean - low) / (limit_eps - fall)
        )
        theta = jnp.clip(theta, 0.0, 1.0)
        return [mean + theta * (value - mean) for value in values]

    def field_after(which, scale, put, arrived):
        from_east, from_west, from_north, from_south = arrived
        later = jnp.stack(unpack_x_high([from_east[which, 0], from_east[which, 1]]))
        earlier = jnp.stack(unpack_x_low([from_west[which, 0], from_west[which, 1]]))
        low, high = trace_x[which, 0], trace_x[which, 1]
        flux = [
            upwind(face_x[0], jnp.where(low_quad, earlier, spin(high[1], 4, 1)), low[0]),
            upwind(face_x[1], high[0], low[1]),
            upwind(face_x[2], high[1], jnp.where(low_quad, spin(low[0], 4, 1), later)),
        ]
        for half in range(2):
            chunk = pl.ds(4 * half, 4)
            low, high = trace_y[which, 0, chunk], trace_y[which, 1, chunk]
            before = jnp.where(first_zone, unpack_y(from_south[which, half], 0), spin(high, 1, 1))
            after = jnp.where(last_zone, unpack_y(from_north[which, half], 3), spin(low, 7, 1))
            lift_y = turned(
                lifts_of(
                    upwind(face_y[0, chunk], before, low), upwind(face_y[1, chunk], high, after)
                )
            )
            lift_x = lifts_of(flux[half], flux[half + 1])
            values = [
                acc_f[which, 4 * half + i] + (lift_x[i] + lift_y[i]) for i in range(4)
            ]
            if scale != 1.0:
                values = [scale * value for value in values]
            values = limited(which, half, values)
            for i in range(4):
                put(4 * half + i, values[i])

    for which in range(3):
        arrange(raw_m, work_m, which)
    for item in range(4):
        mesh_before(item)
    for which in range(2):
        field_ends(which, work_u)
    for which in range(3):
        velocity_before(which, work_v, lambda x: work_v[which, x])
    for copy in first:
        copy.wait_recv()

    def keep_field(x, value):
        sec_f[which, x] = value

    def keep_velocity(x, value):
        sec_v[which, x] = value

    def send_part(part):
        return send_all([ref.at[part] for ref in leaving_b], [ref.at[part] for ref in arrived_b])

    for which in range(3):
        velocity_after(which, keep_velocity, arrived_a)
        pack_velocity(sec_v, which, 2, leaving_b)
    second_v = send_part(pl.ds(2, 3))
    mesh_halo()
    for item in range(4):
        mesh_after(item)
    for which in range(2):
        field_before(which, work_u, lambda x: work_u[which, x])
    for which in range(2):
        field_after(which, 1.0, keep_field, arrived_a)
        field_traces(which, sec_f)
        pack_field(which, which, leaving_b)
    second = send_part(pl.ds(0, 2))

    for which in range(3):
        velocity_before(which, sec_v, lambda x: work_v[which, x] + sec_v[which, x])
    for which in range(2):
        field_ends(which, sec_f)
    for which in range(2):
        field_before(which, sec_f, lambda x: work_u[which, x] + sec_f[which, x])

    def finish_field(x, value):
        for j in range(4):
            results[which, x, pl.ds(j, 8, stride=4), :] = value[j]

    def finish_velocity(x, value):
        for j in range(4):
            results[2 + which, x, pl.ds(j, 8, stride=4), :] = 0.5 * value[j]

    for copy in second_v:
        copy.wait_recv()
    for which in range(3):
        velocity_after(which, finish_velocity, arrived_b)
    for copy in second:
        copy.wait_recv()
    for which in range(2):
        field_after(which, 0.5, finish_field, arrived_b)
    for copy in copies:
        copy.wait_send()


def unfold(results, new_density, new_energy, new_velocity, store_sem):
    copies = []
    for half in range(2):
        rows, block = pl.ds(16 * half, 16), pl.ds(8 * half, 8)
        for source, target in (
            (results.at[0, :, rows, :], new_density.at[block]),
            (results.at[1, :, rows, :], new_energy.at[block]),
            (results.at[pl.ds(2, 3), :, rows, :], new_velocity.at[:, block]),
        ):
            copy = pltpu.make_async_copy(source, target, store_sem.at[len(copies)])
            copy.start()
            copies.append(copy)
    for copy in copies:
        copy.wait()


def solution(mesh):
    counts = (mesh.shape["gx"], mesh.shape["gy"])
    matrices = lane_matrices(128)

    def on_device(*arguments):
        vmem = lambda *shape: pltpu.VMEM(shape, F32)
        scratch = [
            vmem(2, 8, 32, 128), vmem(3, 8, 32, 128), vmem(3, 8, 32, 128),
            vmem(*matrices.shape),
            pltpu.VMEM((256, 512), BF16), pltpu.VMEM((384, 256), BF16),
            pltpu.VMEM((256, 128), BF16), pltpu.VMEM((256, 256), BF16),
            vmem(4, 4, 4, 32), vmem(4, 2, 8, 128), vmem(4, 2, 8, 128),
            vmem(2, 8, 4, 8, 128), vmem(3, 8, 4, 8, 128), vmem(3, 8, 4, 8, 128),
            vmem(3, 8, 4, 8, 128), vmem(3, 8, 4, 8, 128),
            vmem(2, 8, 4, 8, 128), vmem(2, 8, 4, 8, 128),
            vmem(4, 8, 4, 8, 128), vmem(3, 4, 8, 128), vmem(2, 8, 8, 128),
            vmem(2, 2, 2, 4, 8, 128), vmem(2, 2, 8, 8, 128), vmem(2, 2, 256, 128),
            vmem(4, 2, 8, 128), vmem(4, 2, 8, 128), vmem(4, 8, 128),
        ]
        sides = [vmem(items, 2, 8, 128) for items in (8, 5, 8, 5)]
        scratch += sides + sides + [vmem(8, 128)] * 2 + [vmem(5, 2, 8, 128)] * 8
        scratch += [
            pltpu.SemaphoreType.DMA((13,)),
            pltpu.SemaphoreType.DMA((13,)),
            pltpu.SemaphoreType.DMA((13,)),
        ]
        operands = [
            pltpu.with_memory_space_constraint(value, pltpu.HBM)
            for value in (*arguments, jnp.asarray(matrices))
        ]
        results = pl.pallas_call(
            functools.partial(kernel, counts),
            out_shape=pltpu.VMEM((5, 8, 32, 128), F32),
            in_specs=[pl.BlockSpec(memory_space=pltpu.HBM)] * 9,
            out_specs=pl.BlockSpec(memory_space=pltpu.VMEM),
            scratch_shapes=scratch,
            compiler_params=pltpu.CompilerParams(
                collective_id=0, has_side_effects=True, vmem_limit_bytes=32 * 1024 * 1024
            ),
        )(*operands)
        return pl.pallas_call(
            unfold,
            out_shape=[jax.ShapeDtypeStruct(value.shape, F32) for value in arguments[:3]],
            in_specs=[pl.BlockSpec(memory_space=pltpu.VMEM)],
            out_specs=[pl.BlockSpec(memory_space=pltpu.HBM)] * 3,
            scratch_shapes=[pltpu.SemaphoreType.DMA((6,))],
            compiler_params=pltpu.CompilerParams(vmem_limit_bytes=32 * 1024 * 1024),
        )(results)

    fields, vectors = P("gx", "gy", None), P(None, "gx", "gy", None)
    return jax.shard_map(
        on_device,
        mesh=mesh,
        in_specs=(fields, fields, vectors, vectors, fields, fields, fields, fields),
        out_specs=(fields, fields, vectors),
        check_vma=False,
    )
```

profile of v0, /device:TPU:23, one launch (start us, length us, event | category | flops | bytes accessed | tf_op | source)
XLA Modules:
  0.0 24.4 jit_solution(18275968572016655856)
XLA Ops:
  0.6 22.9 %shard_map.112.results = f32[5,8,32,128]{3,2,1,0:T(8,128)S(1)} custom-call(f32[16,16,128]{2,1,0:T(8,128)} %density.1, f32[16,16,128]{2,1,0:T(8,128)} %energy.1, f32[3,16,16,128]{3,2,1,0:T(8,128)} %velocity.1, f32[3,16,16,128]{3,2,1,0:T(8,128)} %mesh_velocity.1, f32[4,4,32]{2,1,0:T(4,128)} %density_low.1, f32[4,4,32]{2,1,0:T(4,128)} %density_high.1, ...), custom_call_target="tpu_custom_call" | custom-call | tf_op jit(solution)/shard_map/pallas_call | solution.py:734
  23.5 0.9 %shard_map.113 = (f32[16,16,128]{2,1,0:T(8,128)}, f32[16,16,128]{2,1,0:T(8,128)}, f32[3,16,16,128]{3,2,1,0:T(8,128)}) custom-call(f32[5,8,32,128]{3,2,1,0:T(8,128)S(1)} %shard_map.112.results), custom_call_target="tpu_custom_call" | custom-call | tf_op jit(solution)/shard_map/pallas_call | solution.py:744
where the time goes:
time: 24.5 us; the launch traced here: 24.4 us
  Pallas kernels  23.8 us (97%)
  between operations  0.64 us (3%)
    pallas_call x1, Pallas kernels, on_device(): pl.pallas_call(functools.partial(kernel, counts), out_shape=pltpu.VMEM((5...  22.9 us
    pallas_call x1, Pallas kernels, on_device(): pl.pallas_call(unfold, out_shape=[jax.ShapeDtypeStruct(value.shape, F32)...  0.88 us

commit v1 on v0

--- a/solution.py
+++ b/solution.py
@@ -268,6 +268,10 @@
     to_south, to_north = (here_x, south), (here_x, north)
     to_corner, from_corner = (west, south), (east, north)
 
+    barrier = pltpu.get_barrier_semaphore()
+    for peer in (to_west, to_east, to_south, to_north, to_corner, from_corner):
+        pl.semaphore_signal(barrier, inc=1, device_id=peer, device_id_type=MESH)
+
     loads = {}
 
     def load(name, source, target):
@@ -281,15 +285,12 @@
 
     places = [(pl.ds(16 * half, 16), pl.ds(8 * half, 8)) for half in range(2)]
     for rows, block in places:
-        load("mesh", mesh_velocity.at[:, block], raw_m.at[:, :, rows, :])
         load("velocity", velocity.at[:, block], raw_v.at[:, :, rows, :])
-    for rows, block in places:
         load("fields", density.at[block], raw_u.at[0, :, rows, :])
         load("fields", energy.at[block], raw_u.at[1, :, rows, :])
-
-    barrier = pltpu.get_barrier_semaphore()
-    for peer in (to_west, to_east, to_south, to_north, to_corner, from_corner):
-        pl.semaphore_signal(barrier, inc=1, device_id=peer, device_id_type=MESH)
+    for rows, block in places:
+        load("mesh", mesh_velocity.at[:, block], raw_m.at[:, :, rows, :])
+
     load("tables", tables_hbm, tables)
     for index, source in enumerate((density_low, density_high, energy_low, energy_high)):
         load("bounds", source, bound_in.at[index])
@@ -300,9 +301,10 @@
     stiff, points = TABLE["stiffness"], TABLE["to_points"]
     zero = jnp.zeros(plane, F32)
 
-    def arrange(source, target, which):
+    def arrange(source, target, which, half):
+        chunk = pl.ds(4 * half, 4)
         for j in range(4):
-            target[which, :, j] = source[which, :, pl.ds(j, 8, stride=4), :]
+            target[which, chunk, j] = source[which, chunk, pl.ds(j, 8, stride=4), :]
 
     def put_pair(target, item, pair):
         target[item, 0] = pair[0]
@@ -320,55 +322,57 @@
     def picked(values):
         return product(sided(values)[1], picker[...])
 
-    def field_traces(which, source):
-        for half in range(2):
-            chunk = pl.ds(4 * half, 4)
-            low, high = traces_of([source[which, 4 * half + i] for i in range(4)])
-            trace_x[which, 0, half], trace_x[which, 1, half] = low, high
-            low, high = traces_of([source[which, chunk, j] for j in range(4)])
-            trace_y[which, 0, chunk], trace_y[which, 1, chunk] = low, high
-
-    def pack_field(which, item, buffers):
-        west_to, east_to, south_to, north_to = buffers
-        put_pair(west_to, item, pack_x_low(trace_x[which, 0, 0]))
-        put_pair(east_to, item, pack_x_high(trace_x[which, 1, 1]))
-        put_pair(south_to, item, pack_y(trace_y[which, 0], 0))
-        put_pair(north_to, item, pack_y(trace_y[which, 1], 3))
-
-    def pack_velocity(source, which, offset, buffers):
-        item = offset + which
-        west_to, east_to, south_to, north_to = buffers
-        put_pair(west_to, item, pack_x_low(source[which, 0]))
-        closing = combine(stiff[4][:4], [source[which, 4 + a] for a in range(4)])
-        put_pair(east_to, item, pack_x_high(closing))
-        put_pair(south_to, item, pack_y(source[which, :, 0], 0))
-        closing = combine(stiff[4][:4], [source[which, :, j] for j in range(4)])
-        put_pair(north_to, item, pack_y(closing, 3))
-
-    leaving_a, leaving_b = (out_dx, out_ux, out_dy, out_uy), (out_dx2, out_ux2, out_dy2, out_uy2)
-    arrived_a, arrived_b = (in_dx, in_ux, in_dy, in_uy), (in_dx2, in_ux2, in_dy2, in_uy2)
+    def traces_along_x(section, which, source, half):
+        low, high = traces_of([source[which, 4 * half + i] for i in range(4)])
+        trace_x[section, which, 0, half], trace_x[section, which, 1, half] = low, high
+
+    def traces_along_y(which, source, half):
+        chunk = pl.ds(4 * half, 4)
+        low, high = traces_of([source[which, chunk, j] for j in range(4)])
+        trace_y[which, 0, chunk], trace_y[which, 1, chunk] = low, high
+
+    def pack_east(section, fields, vectors, target):
+        for which in range(3):
+            closing = combine(stiff[4][:4], [vectors[which, 4 + a] for a in range(4)])
+            put_pair(target, 2 + which, pack_x_high(closing))
+        for which in range(2):
+            traces_along_x(section, which, fields, 1)
+            put_pair(target, which, pack_x_high(trace_x[section, which, 1, 1]))
+
+    def pack_west(section, fields, vectors, target):
+        for which in range(3):
+            put_pair(target, 2 + which, pack_x_low(vectors[which, 0]))
+        for which in range(2):
+            traces_along_x(section, which, fields, 0)
+            put_pair(target, which, pack_x_low(trace_x[section, which, 0, 0]))
+
+    def pack_south_north(fields, vectors, south_to, north_to):
+        for which in range(2):
+            for half in range(2):
+                traces_along_y(which, fields, half)
+            put_pair(south_to, which, pack_y(trace_y[which, 0], 0))
+            put_pair(north_to, which, pack_y(trace_y[which, 1], 3))
+        for which in range(3):
+            put_pair(south_to, 2 + which, pack_y(vectors[which, :, 0], 0))
+            closing = combine(stiff[4][:4], [vectors[which, :, j] for j in range(4)])
+            put_pair(north_to, 2 + which, pack_y(closing, 3))
+
+    loaded("velocity")
+    loaded("fields")
+    for half in (1, 0):
+        for which in range(3):
+            arrange(raw_v, work_v, which, half)
+        for which in range(2):
+            arrange(raw_u, work_u, which, half)
+    pack_east(0, work_u, work_v, out_ux)
+    pack_west(0, work_u, work_v, out_dx)
     loaded("mesh")
-    corner = zero
     for which in range(3):
-        values = raw_m[which, :, pl.ds(0, 8, stride=4), :]
-        put_pair(out_dy, 5 + which, pack_y(values, 0))
-        corner = jnp.where(rows_of(plane) == which, spin(values[0], which, 0), corner)
         values = [raw_m[which, 0, pl.ds(j, 8, stride=4), :] for j in range(4)]
         put_pair(out_dx, 5 + which, pack_x_low(values))
-    out_corner[...] = corner
-    loaded("velocity")
-    for which in range(3):
-        arrange(raw_v, work_v, which)
-        pack_velocity(work_v, which, 2, leaving_a)
-    loaded("fields")
-    for which in range(2):
-        arrange(raw_u, work_u, which)
-        field_traces(which, work_u)
-        pack_field(which, which, leaving_a)
 
     pl.semaphore_wait(barrier, 6)
     copies = []
-    peers = (to_west, to_east, to_south, to_north)
 
     def send(source, target, peer):
         copy = pltpu.make_async_remote_copy(
@@ -380,10 +384,21 @@
         copies.append(copy)
         return copy
 
-    def send_all(sources, targets):
-        return [send(*triple) for triple in zip(sources, targets, peers)]
-
-    first = send_all(leaving_a, arrived_a) + [send(out_corner, in_corner, to_corner)]
+    first_ux = send(out_ux, in_ux, to_east)
+    first = [send(out_dx, in_dx, to_west)]
+    pack_south_north(work_u, work_v, out_dy, out_uy)
+    corner = zero
+    for which in range(3):
+        values = raw_m[which, :, pl.ds(0, 8, stride=4), :]
+        put_pair(out_dy, 5 + which, pack_y(values, 0))
+        corner = jnp.where(rows_of(plane) == which, spin(values[0], which, 0), corner)
+    out_corner[...] = corner
+    first += [
+        send(out_corner, in_corner, to_corner),
+        send(out_dy, in_dy, to_south),
+        send(out_uy, in_uy, to_north),
+    ]
+    arrived_a, arrived_b = (in_dx, in_ux, in_dy, in_uy), (in_dx2, in_ux2, in_dy2, in_uy2)
 
     loaded("tables")
     minus, plus, stiff_z, interp_z, pick_z, spread_z, volume_z, lift_z = (
@@ -451,26 +466,28 @@
                     + work_m[2, x] * along_z[x]
                 )
 
-    def velocity_after(which, put, arrived):
+    def velocity_after(which, half, put, arrived):
         from_east, from_west, from_north, from_south = arrived
-        later = jnp.stack(unpack_x_high([from_east[2 + which, 0], from_east[2 + which, 1]]))
-        earlier = jnp.stack(unpack_x_low([from_west[2 + which, 0], from_west[2 + which, 1]]))
-        later = jnp.where(low_quad, 0.0, later)
-        earlier = jnp.where(low_quad, earlier, 0.0)
-        for half in range(2):
-            above = jnp.where(last_zone, unpack_y(from_north[2 + which, half], 3), 0.0)
-            below = jnp.where(first_zone, unpack_y(from_south[2 + which, half], 0), 0.0)
-            extra_y = [stiff[j][4] * above for j in range(4)]
-            extra_y[0] = extra_y[0] + below
-            extra_y = turned(extra_y)
-            for a in range(4):
-                x = 4 * half + a
-                value = acc_v[which, x] + work_m[1, x] * extra_y[a]
-                if half == 1:
-                    value = value + work_m[0, x] * (stiff[a][4] * later)
-                elif a == 0:
-                    value = value + work_m[0, x] * earlier
-                put(x, value)
+        item = 2 + which
+        above = jnp.where(last_zone, unpack_y(from_north[item, half], 3), 0.0)
+        below = jnp.where(first_zone, unpack_y(from_south[item, half], 0), 0.0)
+        extra_y = [stiff[j][4] * above for j in range(4)]
+        extra_y[0] = extra_y[0] + below
+        extra_y = turned(extra_y)
+        if half == 1:
+            later = jnp.stack(unpack_x_high([from_east[item, 0], from_east[item, 1]]))
+            later = jnp.where(low_quad, 0.0, later)
+        else:
+            earlier = jnp.stack(unpack_x_low([from_west[item, 0], from_west[item, 1]]))
+            earlier = jnp.where(low_quad, earlier, 0.0)
+        for a in range(4):
+            x = 4 * half + a
+            value = acc_v[which, x] + work_m[1, x] * extra_y[a]
+            if half == 1:
+                value = value + work_m[0, x] * (stiff[a][4] * later)
+            elif a == 0:
+                value = value + work_m[0, x] * earlier
+            put(x, value)
 
     def mesh_before(item):
         values = work_m[min(item, 2)].reshape(256, 128)
@@ -505,37 +522,38 @@
             halo_y[item] = source[48 + 16 * which : 64 + 16 * which].reshape(2, 8, 128)
             halo_corner[item] = spin(source[96:104], 7 - which, 0)
 
-    def mesh_after(item):
+    def mesh_after(item, half):
         rows = rows_of(plane)
-        later = unpack_x_high([halo_x[item, 0], halo_x[item, 1]])
-        later = [jnp.where(low_rows, 0.0, value) for value in later]
-        far = jnp.where(at_zone(plane, 3), 0.0, spin(later[0], 7, 0))
-        far = jnp.where(rows == 7, halo_corner[item], far)
-        later.append(jnp.where(low_rows, 0.0, far))
-        edge = jnp.stack(points_of(points, later))
-        above = [
-            jnp.where(last_zone, unpack_y(halo_y[item, half], 3), 0.0) for half in range(2)
-        ]
-        inner = jnp.where(low_rows, spin(above[0][0], 4, 0), 0.0)
-        for half in range(2):
-            ahead = above[1][0] if half == 0 else inner
-            across = points_of(points, [above[half][a] for a in range(4)] + [ahead])
-            for i in range(4):
-                x = 4 * half + i
-                extra = jnp.stack([points[j][4] * across[i] for j in range(4)])
+        above = jnp.where(last_zone, unpack_y(halo_y[item, half], 3), 0.0)
+        if half == 1:
+            first_above = jnp.where(at_zone(plane, 3), spin(halo_y[item, 0], 3, 0), 0.0)
+            ahead = jnp.where(low_rows, spin(first_above, 4, 0), 0.0)
+            later = unpack_x_high([halo_x[item, 0], halo_x[item, 1]])
+            later = [jnp.where(low_rows, 0.0, value) for value in later]
+            far = jnp.where(at_zone(plane, 3), 0.0, spin(later[0], 7, 0))
+            far = jnp.where(rows == 7, halo_corner[item], far)
+            later.append(jnp.where(low_rows, 0.0, far))
+            edge = jnp.stack(points_of(points, later))
+        else:
+            ahead = jnp.where(at_zone(plane, 3), spin(halo_y[item, 1], 3, 0), 0.0)
+        across = points_of(points, [above[a] for a in range(4)] + [ahead])
+        for i in range(4):
+            x = 4 * half + i
+            extra = jnp.stack([points[j][4] * across[i] for j in range(4)])
+            if half == 1:
+                extra = extra + points[i][4] * edge
+            speed[item, x] += extra
+            if item == 1:
+                upper = face_y[1, x] + across[i]
                 if half == 1:
-                    extra = extra + points[i][4] * edge
-                speed[item, x] += extra
-                if item == 1:
-                    upper = face_y[1, x] + across[i]
-                    if half == 1:
-                        upper = upper + points[i][4] * later[4]
-                        face_y[0, x] += points[i][4] * later[0]
-                    face_y[1, x] = upper
-            if item == 0:
-                face_x[half] += jnp.stack([points[j][4] * above[half][0] for j in range(4)])
+                    upper = upper + points[i][4] * later[4]
+                    face_y[0, x] += points[i][4] * later[0]
+                face_y[1, x] = upper
         if item == 0:
-            face_x[2] = jnp.where(low_quad, spin(face_x[0], 4, 1), edge)
+            face_x[half] += jnp.stack([points[j][4] * above[0] for j in range(4)])
+            if half == 1:
+                lowest = face_x[0] + jnp.stack([points[j][4] * first_above for j in range(4)])
+                face_x[2] = jnp.where(low_quad, spin(lowest, 4, 1), edge)
 
     def upwind(face, minus_side, plus_side):
         return jnp.maximum(face, 0.0) * minus_side + jnp.minimum(face, 0.0) * plus_side
@@ -546,25 +564,26 @@
         ends_z[which, 0] = sides[:, :128]
         ends_z[which, 1] = sides[:, 128:]
 
-    def field_before(which, source, base):
-        values = source[which].reshape(256, 128)
-        flux = upwind(speed[3].reshape(256, 128), ends_z[which, 0], ends_z[which, 1])
-        moved = speed[2].reshape(256, 128) * values
+    def field_before(which, half, source, base):
+        chunk, rows = pl.ds(4 * half, 4), pl.ds(128 * half, 128)
+        values = source[which, chunk].reshape(128, 128)
+        flux = upwind(
+            speed[3, chunk].reshape(128, 128), ends_z[which, 0, rows], ends_z[which, 1, rows]
+        )
+        moved = speed[2, chunk].reshape(128, 128) * values
         upper, lower = parted(jnp.concatenate([moved, flux], 1))
         sums = product(upper, tall[...])
         along_z = sums[:, :128] + sums[:, 128:] + product(lower, tall[:, :128])
-        along_z = along_z.reshape(8, 4, 8, 128)
-        for half in range(2):
-            chunk = pl.ds(4 * half, 4)
-            places = [4 * half + i for i in range(4)]
-            along_x = slopes_of(TABLE["volume"], [speed[0, x] * source[which, x] for x in places])
-            along_y = slopes_of(
-                TABLE["volume"],
-                [speed[1, chunk, j] * source[which, chunk, j] for j in range(4)],
-            )
-            along_y = turned(along_y)
-            for i, x in enumerate(places):
-                acc_f[which, x] = base(x) + ((along_x[i] + along_y[i]) + along_z[x])
+        along_z = along_z.reshape(4, 4, 8, 128)
+        places = [4 * half + i for i in range(4)]
+        along_x = slopes_of(TABLE["volume"], [speed[0, x] * source[which, x] for x in places])
+        along_y = slopes_of(
+            TABLE["volume"],
+            [speed[1, chunk, j] * source[which, chunk, j] for j in range(4)],
+        )
+        along_y = turned(along_y)
+        for i, x in enumerate(places):
+            acc_f[which, x] = base(x) + ((along_x[i] + along_y[i]) + along_z[i])
 
     def in_group(values, join):
         lane = lax.broadcasted_iota(jnp.int32, plane, 1)
@@ -593,94 +612,95 @@
         theta = jnp.clip(theta, 0.0, 1.0)
         return [mean + theta * (value - mean) for value in values]
 
-    def field_after(which, scale, put, arrived):
+    def field_after(section, which, half, put, arrived):
         from_east, from_west, from_north, from_south = arrived
-        later = jnp.stack(unpack_x_high([from_east[which, 0], from_east[which, 1]]))
-        earlier = jnp.stack(unpack_x_low([from_west[which, 0], from_west[which, 1]]))
-        low, high = trace_x[which, 0], trace_x[which, 1]
-        flux = [
-            upwind(face_x[0], jnp.where(low_quad, earlier, spin(high[1], 4, 1)), low[0]),
-            upwind(face_x[1], high[0], low[1]),
-            upwind(face_x[2], high[1], jnp.where(low_quad, spin(low[0], 4, 1), later)),
-        ]
+        low, high = trace_x[section, which, 0], trace_x[section, which, 1]
+        flux = [None, upwind(face_x[1], high[0], low[1]), None]
+        if half == 1:
+            later = jnp.stack(unpack_x_high([from_east[which, 0], from_east[which, 1]]))
+            later = jnp.where(low_quad, spin(low[0], 4, 1), later)
+            flux[2] = upwind(face_x[2], high[1], later)
+        else:
+            earlier = jnp.stack(unpack_x_low([from_west[which, 0], from_west[which, 1]]))
+            earlier = jnp.where(low_quad, earlier, spin(high[1], 4, 1))
+            flux[0] = upwind(face_x[0], earlier, low[0])
+        chunk = pl.ds(4 * half, 4)
+        low, high = trace_y[which, 0, chunk], trace_y[which, 1, chunk]
+        before = jnp.where(first_zone, unpack_y(from_south[which, half], 0), spin(high, 1, 1))
+        after = jnp.where(last_zone, unpack_y(from_north[which, half], 3), spin(low, 7, 1))
+        lift_y = turned(
+            lifts_of(upwind(face_y[0, chunk], before, low), upwind(face_y[1, chunk], high, after))
+        )
+        lift_x = lifts_of(flux[half], flux[half + 1])
+        values = [acc_f[which, 4 * half + i] + (lift_x[i] + lift_y[i]) for i in range(4)]
+        if section == 1:
+            values = [0.5 * value for value in values]
+        values = limited(which, half, values)
+        for i in range(4):
+            put(4 * half + i, values[i])
+
+    for which in range(3):
         for half in range(2):
-            chunk = pl.ds(4 * half, 4)
-            low, high = trace_y[which, 0, chunk], trace_y[which, 1, chunk]
-            before = jnp.where(first_zone, unpack_y(from_south[which, half], 0), spin(high, 1, 1))
-            after = jnp.where(last_zone, unpack_y(from_north[which, half], 3), spin(low, 7, 1))
-            lift_y = turned(
-                lifts_of(
-                    upwind(face_y[0, chunk], before, low), upwind(face_y[1, chunk], high, after)
-                )
-            )
-            lift_x = lifts_of(flux[half], flux[half + 1])
-            values = [
-                acc_f[which, 4 * half + i] + (lift_x[i] + lift_y[i]) for i in range(4)
-            ]
-            if scale != 1.0:
-                values = [scale * value for value in values]
-            values = limited(which, half, values)
-            for i in range(4):
-                put(4 * half + i, values[i])
-
-    for which in range(3):
-        arrange(raw_m, work_m, which)
+            arrange(raw_m, work_m, which, half)
     for item in range(4):
         mesh_before(item)
     for which in range(2):
         field_ends(which, work_u)
     for which in range(3):
         velocity_before(which, work_v, lambda x: work_v[which, x])
+
+    def keep_field(x, value):
+        sec_f[which, x] = value
+
+    def keep_velocity(x, value):
+        sec_v[which, x] = value
+
+    def finish_field(x, value):
+        for j in range(4):
+            results[which, x, pl.ds(j, 8, stride=4), :] = value[j]
+
+    def finish_velocity(x, value):
+        for j in range(4):
+            results[2 + which, x, pl.ds(j, 8, stride=4), :] = 0.5 * value[j]
+
     for copy in first:
         copy.wait_recv()
-
-    def keep_field(x, value):
-        sec_f[which, x] = value
-
-    def keep_velocity(x, value):
-        sec_v[which, x] = value
-
-    def send_part(part):
-        return send_all([ref.at[part] for ref in leaving_b], [ref.at[part] for ref in arrived_b])
-
-    for which in range(3):
-        velocity_after(which, keep_velocity, arrived_a)
-        pack_velocity(sec_v, which, 2, leaving_b)
-    second_v = send_part(pl.ds(2, 3))
     mesh_halo()
-    for item in range(4):
-        mesh_after(item)
-    for which in range(2):
-        field_before(which, work_u, lambda x: work_u[which, x])
-    for which in range(2):
-        field_after(which, 1.0, keep_field, arrived_a)
-        field_traces(which, sec_f)
-        pack_field(which, which, leaving_b)
-    second = send_part(pl.ds(0, 2))
+    for half in (1, 0):
+        if half == 0:
+            first_ux.wait_recv()
+        for item in range(4):
+            mesh_after(item, half)
+        for which in range(2):
+            field_before(which, half, work_u, lambda x: work_u[which, x])
+        for which in range(3):
+            velocity_after(which, half, keep_velocity, arrived_a)
+        for which in range(2):
+            field_after(0, which, half, keep_field, arrived_a)
+        if half == 1:
+            pack_east(1, sec_f, sec_v, out_ux2)
+            second_ux = send(out_ux2, in_ux2, to_east)
+    pack_west(1, sec_f, sec_v, out_dx2)
+    second = [send(out_dx2, in_dx2, to_west)]
+    pack_south_north(sec_f, sec_v, out_dy2, out_uy2)
+    second += [send(out_dy2, in_dy2, to_south), send(out_uy2, in_uy2, to_north)]
 
     for which in range(3):
         velocity_before(which, sec_v, lambda x: work_v[which, x] + sec_v[which, x])
     for which in range(2):
         field_ends(which, sec_f)
     for which in range(2):
-        field_before(which, sec_f, lambda x: work_u[which, x] + sec_f[which, x])
-
-    def finish_field(x, value):
-        for j in range(4):
-            results[which, x, pl.ds(j, 8, stride=4), :] = value[j]
-
-    def finish_velocity(x, value):
-        for j in range(4):
-            results[2 + which, x, pl.ds(j, 8, stride=4), :] = 0.5 * value[j]
-
-    for copy in second_v:
-        copy.wait_recv()
-    for which in range(3):
-        velocity_after(which, finish_velocity, arrived_b)
+        for half in range(2):
+            field_before(which, half, sec_f, lambda x: work_u[which, x] + sec_f[which, x])
     for copy in second:
         copy.wait_recv()
-    for which in range(2):
-        field_after(which, 0.5, finish_field, arrived_b)
+    for half in (1, 0):
+        if half == 0:
+            second_ux.wait_recv()
+        for which in range(3):
+            velocity_after(which, half, finish_velocity, arrived_b)
+        for which in range(2):
+            field_after(1, which, half, finish_field, arrived_b)
     for copy in copies:
         copy.wait_send()
 
@@ -717,7 +737,7 @@
             vmem(3, 8, 4, 8, 128), vmem(3, 8, 4, 8, 128),
             vmem(2, 8, 4, 8, 128), vmem(2, 8, 4, 8, 128),
             vmem(4, 8, 4, 8, 128), vmem(3, 4, 8, 128), vmem(2, 8, 8, 128),
-            vmem(2, 2, 2, 4, 8, 128), vmem(2, 2, 8, 8, 128), vmem(2, 2, 256, 128),
+            vmem(2, 2, 2, 2, 4, 8, 128), vmem(2, 2, 8, 8, 128), vmem(2, 2, 256, 128),
             vmem(4, 2, 8, 128), vmem(4, 2, 8, 128), vmem(4, 8, 128),
         ]
         sides = [vmem(items, 2, 8, 128) for items in (8, 5, 8, 5)]

time: 24.5 us -> 24.7 us (level)
  the two profiles are of different devices: /device:TPU:23 before, /device:TPU:7 now
where the time goes in v1:
time: 24.7 us; the launch traced here: 24.6 us
  Pallas kernels  23.9 us (97%)
  between operations  0.64 us (3%)
    pallas_call x1, Pallas kernels, on_device(): pl.pallas_call(functools.partial(kernel, counts), out_shape=pltpu.VMEM((5...  23 us
    pallas_call x1, Pallas kernels, on_device(): pl.pallas_call(unfold, out_shape=[jax.ShapeDtypeStruct(value.shape, F32)...  0.88 us

profile of v1, /device:TPU:7, one launch (start us, length us, event | category | flops | bytes accessed | tf_op | source)
XLA Modules:
  0.0 24.6 jit_solution(14143190683528088974)
XLA Ops:
  0.6 23.0 %shard_map.112.results = f32[5,8,32,128]{3,2,1,0:T(8,128)S(1)} custom-call(f32[16,16,128]{2,1,0:T(8,128)} %density.1, f32[16,16,128]{2,1,0:T(8,128)} %energy.1, f32[3,16,16,128]{3,2,1,0:T(8,128)} %velocity.1, f32[3,16,16,128]{3,2,1,0:T(8,128)} %mesh_velocity.1, f32[4,4,32]{2,1,0:T(4,128)} %density_low.1, f32[4,4,32]{2,1,0:T(4,128)} %density_high.1, ...), custom_call_target="tpu_custom_call" | custom-call | tf_op jit(solution)/shard_map/pallas_call | solution.py:754
  23.7 0.9 %shard_map.113 = (f32[16,16,128]{2,1,0:T(8,128)}, f32[16,16,128]{2,1,0:T(8,128)}, f32[3,16,16,128]{3,2,1,0:T(8,128)}) custom-call(f32[5,8,32,128]{3,2,1,0:T(8,128)S(1)} %shard_map.112.results), custom_call_target="tpu_custom_call" | custom-call | tf_op jit(solution)/shard_map/pallas_call | solution.py:764
